TPU v7x, 32 devices: a whole 2x2x4 slice. The times are simulated.
32 devices in a mesh: rec: 4 (over z), tm: 8 (over y, x, core).
Axes of the slice: x: 2, y: 2, z: 4, core: 2. Of those that a mesh axis runs over, the one named last changes fastest.
Arguments:
- audio: float32 [4, 40960], P('rec', 'tm'), may hold values from -100 to 100, as said below
- conv0_weight: float32 [10, 512], replicated, may hold values from -2 to 2
- norm_gain: float32 [512], replicated, may hold values from 0.25 to 1.75
- norm_bias: float32 [512], replicated, may hold values from -3 to 3
- conv1_weight: bfloat16 [1536, 512], replicated, may hold values from -0.25 to 0.25
- conv2_weight: bfloat16 [1536, 512], replicated, may hold values from -0.25 to 0.25
- cotangent: bfloat16 [4, 2048, 512], P('rec', 'tm'), may hold values from -0.09375 to 0.09375
Outputs:
- features: bfloat16 [4, 2048, 512], P('rec', 'tm')
- grad_conv0: float32 [10, 512], replicated
- grad_gain: float32 [512], replicated
- grad_bias: float32 [512], replicated
- grad_conv1: float32 [1536, 512], replicated
- grad_conv2: float32 [1536, 512], replicated
Inputs may be any that keep to these rules, and one draw needn't show every extreme that they name: `audio`: recorded waveforms, one row a recording.
All inputs are finite; a program needn't handle non-finite values.
Results may differ from a plain program's by a relative error of at most 0.0095.
Values may be sent and summed in bfloat16 or wider, within the bound.
A program may use at most 64 MiB of HBM per device.

v0:
```python
import jax
import jax.numpy as jnp
from jax import lax
from jax.sharding import PartitionSpec as P

EPS = 1e-05
HIGH = lax.Precision.HIGHEST


def from_behind(value, axis, steps):
    count = lax.axis_size(axis)
    leading, last = (max(0, -steps), min(count, count - steps))
    return lax.ppermute(value, axis, [(source, source + steps) for source in range(leading, last)])


def gelu_slope(value):
    return (
        0.5 * (1.0 + lax.erf(value * 0.7071067811865476))
        + value * jnp.exp(-0.5 * value * value) * 0.3989422804014327
    )


def stride_conv(active, weight):
    records, frames_in, channels = active.shape
    edge_row = from_behind(active[:, :1, :], "tm", -1)
    pairs = active.reshape(records, frames_in // 2, 2 * channels)
    following = jnp.concatenate([pairs[:, 1:, :channels], edge_row], 1)
    output = jnp.einsum(
        "rtk,kc->rtc", pairs, weight[: 2 * channels], preferred_element_type=jnp.float32
    )
    output = output + jnp.einsum(
        "rtk,kc->rtc", following, weight[2 * channels :], preferred_element_type=jnp.float32
    )
    return (pairs, following, output)


def weight_grad(pairs, following, delta):
    upper = jnp.einsum("rtk,rtc->kc", pairs, delta, preferred_element_type=jnp.float32)
    lower = jnp.einsum("rtk,rtc->kc", following, delta, preferred_element_type=jnp.float32)
    return jnp.concatenate([upper, lower], 0)


def stride_back(delta, weight):
    records, frames_out, channels = delta.shape
    edge_row = from_behind(delta[:, -1:, :], "tm", 1)
    before = jnp.concatenate([edge_row, delta[:, :-1, :]], 1)
    back_pairs = jnp.einsum(
        "rtc,kc->rtk", delta, weight[: 2 * channels], preferred_element_type=jnp.float32
    )
    shifted = jnp.einsum(
        "rtc,kc->rtk", before, weight[2 * channels :], preferred_element_type=jnp.float32
    )
    even_rows = back_pairs[:, :, :channels] + shifted
    joined = jnp.concatenate([even_rows, back_pairs[:, :, channels:]], 2)
    return joined.reshape(records, 2 * frames_out, channels)


def shards(audio, conv0_weight, norm_gain, norm_bias, conv1_weight, conv2_weight, cotangent):
    records = audio.shape[0]
    blocks = audio.reshape(records, audio.shape[1] // 5, 5)
    count = float(blocks.shape[1] * lax.axis_size("tm"))
    sample_edge = from_behind(blocks[:, :1, :], "tm", -1)
    following = jnp.concatenate([blocks[:, 1:, :], sample_edge], 1)
    patches = jnp.concatenate([blocks, following], 2)
    pre_norm = jnp.einsum("rtk,kc->rtc", patches, conv0_weight, precision=HIGH)
    first, second = lax.psum((jnp.sum(pre_norm, 1), jnp.sum(pre_norm * pre_norm, 1)), "tm")
    mean = first / count
    variance = second / count - mean * mean
    centered = pre_norm - mean[:, None, :]
    inverse = lax.rsqrt(variance + EPS)
    normed = centered * inverse[:, None, :]
    shifted_norm = normed * norm_gain + norm_bias
    act0 = jax.nn.gelu(shifted_norm, approximate=False).astype(jnp.bfloat16)
    pairs1, follow1, pre1 = stride_conv(act0, conv1_weight)
    act1 = jax.nn.gelu(pre1, approximate=False).astype(jnp.bfloat16)
    pairs2, follow2, pre2 = stride_conv(act1, conv2_weight)
    features = jax.nn.gelu(pre2, approximate=False).astype(jnp.bfloat16)
    delta2 = (cotangent.astype(jnp.float32) * gelu_slope(pre2)).astype(jnp.bfloat16)
    grad_two = weight_grad(pairs2, follow2, delta2)
    back1 = stride_back(delta2, conv2_weight)
    delta1 = (back1 * gelu_slope(pre1)).astype(jnp.bfloat16)
    grad_one = weight_grad(pairs1, follow1, delta1)
    back0 = stride_back(delta1, conv1_weight)
    dnorm = back0 * gelu_slope(shifted_norm)
    local_one = jnp.sum(dnorm, 1)
    local_two = jnp.sum(dnorm * normed, 1)
    sum_one, sum_two = lax.psum((local_one, local_two), "tm")
    scale = norm_gain * inverse
    dpre = scale[:, None, :] * (
        dnorm - (sum_one / count)[:, None, :] - normed * (sum_two / count)[:, None, :]
    )
    grad_zero = jnp.einsum("rtk,rtc->kc", patches, dpre, precision=HIGH)
    norm_terms = jnp.stack([jnp.sum(local_two, 0), jnp.sum(local_one, 0)], 0)
    grad_zero, norm_terms, grad_one, grad_two = lax.psum(
        (grad_zero, norm_terms, grad_one, grad_two), ("rec", "tm")
    )
    return (features, grad_zero, norm_terms[0], norm_terms[1], grad_one, grad_two)


def solution(mesh):
    return jax.shard_map(
        shards,
        mesh=mesh,
        in_specs=(P("rec", "tm"), P(), P(), P(), P(), P(), P("rec", "tm", None)),
        out_specs=(P("rec", "tm", None), P(), P(), P(), P(), P()),
        check_vma=False,
    )
```

profile of v0, /device:TPU:0, one launch (start us, length us, event | category | flops | bytes accessed | tf_op | source)
XLA Modules:
  0.0 249.6 jit_solution(3588708600532290643)
XLA Ops:
  7.2 0.0 copy-start
  7.2 0.0 all-reduce.6.cloned.1.call-start
  7.2 0.5 broadcast.213
  7.7 1.4 reduce.11
  9.2 0.4 reshape.355
  9.5 0.0 copy-start.7
  9.5 0.0 copy-start.8
  9.6 1.3 collective-permute-start
  10.9 0.2 copy.17
  11.1 0.2 copy.15
  11.3 1.3 collective-permute-done
  12.6 0.1 copy.16
  12.7 0.1 maximum_maximum_fusion
  12.8 1.9 fusion.93
  14.7 15.5 %all-reduce.3 = (f32[1,512]{1,0:T(1,128)S(1)}, f32[1,512]{1,0:T(1,128)S(1)}) all-reduce(f32[1,512]{1,0:T(1,128)S(1)} %bitcast.99, f32[1,512]{1,0:T(1,128)S(1)} %bitcast.98), channel_id=1, replica_groups=mesh['rec'=4,'tm'=8] {'tm'}, use_global_device_ids=true, to_apply=%region_3.0 | all-reduce | flops 1024 | bytes 8192 | tf_op jit(solution)/shard_map/psum | solution.py:66
  30.2 4.9 %fusion.2 = bf16[1024,512]{1,0:T(8,128)(2,1)S(1)} fusion(f32[1024,512]{1,0:T(8,128)S(1)} %get-tuple-element.24, f32[512]{0:T(512)S(1)} %copy-done.8, f32[512]{0:T(512)S(1)} %copy-done.7, f32[512]{0:T(512)S(1)} %bitcast.82, f32[512]{0:T(512)S(1)} %bitcast.86), kind=kLoop, calls=%fused_computation.6 | loop fusion | flops 36175872 | bytes 3153920 | tf_op jit(solution)/shard_map/convert_element_type | solution.py:73
  35.2 5.7 %fusion.106 = bf16[1,1024,512]{2,1,0:T(8,128)(2,1)} fusion(f32[512]{0:T(512)S(1)} %copy-done.8, f32[512]{0:T(512)S(1)} %copy-done.7, f32[512]{0:T(512)S(1)} %bitcast.83, f32[1024,512]{1,0:T(8,128)S(1)} %get-tuple-element.24, f32[512]{0:T(512)S(1)} %bitcast.87), kind=kLoop, calls=%fused_computation.151 | loop fusion | flops 36175872 | bytes 3153920 | tf_op jit(solution)/shard_map/convert_element_type | solution.py:73
  40.8 1.1 reshape.357
  42.0 0.7 slice.87
  42.7 1.3 collective-permute-start.1
  44.0 3.2 %fusion.47 = f32[512,512]{1,0:T(8,128)} fusion(bf16[512,1024]{1,0:T(8,128)(2,1)} %reshape.357, bf16[1536,512]{1,0:T(8,128)(2,1)} %param.11), kind=kOutput, calls=%fused_computation.81 | convolution fusion | flops 536870912 | bytes 3145728 | tf_op jit(solution)/shard_map/rtk,kc->rtc/dot_general | solution.py:28
  47.2 1.1 reshape.358
  48.3 1.2 slice.86
  49.5 0.0 collective-permute-done.1
  49.5 4.9 %fusion.24 = (bf16[512,512]{1,0:T(8,128)(2,1)S(1)}, f32[512,512]{1,0:T(8,128)}) fusion(f32[512,512]{1,0:T(8,128)} %fusion.47, bf16[1536,512]{1,0:T(8,128)(2,1)} %param.11, bf16[1,1,512]{2,1,0:T(2,128)(2,1)S(1)} %collective-permute-done.1, bf16[1,511,512]{2,1,0:T(8,128)(2,1)S(1)} %slice.86), kind=kOutput, calls=%fused_computation.49 | convolution fusion | flops 286785536 | bytes 3670016 | tf_op jit(solution)/shard_map/rtk,kc->rtc/dot_general | solution.py:31
  54.5 0.2 reshape.360
  54.6 0.0 copy-start.9
  54.7 1.4 collective-permute-start.2
  56.1 2.5 fusion.44
  58.6 1.0 reshape.361
  59.5 1.0 slice.88
  60.6 0.0 collective-permute-done.2
  60.6 2.5 fusion.58
  63.1 0.5 fusion.77
  63.5 3.8 %collective-permute-start.3 = (bf16[1,1,512]{2,1,0:T(2,128)(2,1)S(1)}, bf16[1,1,512]{2,1,0:T(2,128)(2,1)S(1)}, u32[]{:S(2)}, u32[]{:S(2)}) collective-permute-start(bf16[1,1,512]{2,1,0:T(2,128)(2,1)S(1)} %slice.91), channel_id=1, source_target_pairs={{0,1},{1,2},{2,3},{3,4},{4,5},{5,6},{6,7},{8,9},{9,10},{10,11},{11... | collective-permute-start | bytes 3080 | tf_op jit(solution)/shard_map/ppermute | solution.py:13
  67.4 0.3 fusion.75
  67.7 0.0 copy-start.3
  67.7 2.0 pad_maximum_fusion.1
  69.7 0.5 convolution_bitcast_fusion.2
  70.2 0.3 fusion.21
  70.6 0.1 pad_maximum_fusion.3
  70.7 1.2 reshape.365
  71.8 2.1 fusion.30
  73.9 0.7 fusion.97
  74.7 0.3 copy-done.6
  75.0 0.5 fusion.72
  75.4 2.0 pad_maximum_fusion
  77.4 0.0 all-reduce.6.cloned.1.call-update
  77.4 1.0 copy-done.4
  78.4 1.8 fusion.80
  80.3 3.6 %collective-permute-start.4 = (bf16[1,1,512]{2,1,0:T(2,128)(2,1)S(1)}, bf16[1,1,512]{2,1,0:T(2,128)(2,1)S(1)}, u32[]{:S(2)}, u32[]{:S(2)}) collective-permute-start(bf16[1,1,512]{2,1,0:T(2,128)(2,1)S(1)} %slice.95), channel_id=1, source_target_pairs={{0,1},{1,2},{2,3},{3,4},{4,5},{5,6},{6,7},{8,9},{9,10},{10,11},{11... | collective-permute-start | bytes 3080 | tf_op jit(solution)/shard_map/ppermute | solution.py:13
  83.9 2.0 convolution_bitcast_fusion
  85.9 0.1 slice.97
  86.0 1.6 fusion.20
  87.6 1.5 pad_maximum_fusion.2
  89.0 2.8 %reshape.367 = f32[1024,512]{1,0:T(8,128)} reshape(f32[1,512,1024]{2,1,0:T(8,128)} %pad_maximum_fusion.2) | data formatting | bytes 4194304 | tf_op jit(solution)/shard_map/reshape | solution.py:55
  91.8 3.6 %fusion.92 = (f32[512]{0:T(512)S(1)}, f32[512]{0:T(512)S(1)}, f32[1024,512]{1,0:T(8,128)}) fusion(f32[512]{0:T(512)S(1)} %bitcast.84, f32[1024,512]{1,0:T(8,128)S(1)} %get-tuple-element.24, f32[512]{0:T(512)S(1)} %bitcast.88, f32[1024,512]{1,0:T(8,128)} %reshape.367, f32[512]{0:T(512)S(1)} %copy-done.8, f32[512]{0:T(512)S(1)} %copy-done.7), kind=kLoop, calls=%fused_computation.146 | loop fusion | flops 8387584 | bytes 6303744 | tf_op jit(solution)/shard_map/reduce_sum | solution.py:85
  95.4 12.9 %all-reduce.2 = (f32[1,512]{1,0:T(1,128)S(1)}, f32[1,512]{1,0:T(1,128)S(1)}) all-reduce(f32[1,512]{1,0:T(1,128)S(1)} %bitcast.93, f32[1,512]{1,0:T(1,128)S(1)} %bitcast.91), channel_id=1, replica_groups=mesh['rec'=4,'tm'=8] {'tm'}, use_global_device_ids=true, to_apply=%region_7.0 | all-reduce | flops 1024 | bytes 8192 | tf_op jit(solution)/shard_map/psum | solution.py:87
  108.3 3.1 %fusion.8 = f32[10,512]{1,0:T(8,128)S(1)} fusion(f32[1024,512]{1,0:T(8,128)} %get-tuple-element.20, f32[1024,512]{1,0:T(8,128)S(1)} %get-tuple-element.24, f32[512]{0:T(512)S(1)} %bitcast.96, f32[512]{0:T(512)S(1)} %bitcast.97, f32[512]{0:T(512)S(1)} %bitcast.95, f32[512]{0:T(512)S(1)} %bitcast.85, f32[512]{0:T(512)S(1)} %bitcast.89, ...), kind=kOutput, calls=%fused_computation.13 | convolution fusion | flops 66060288 | bytes 4265984 | tf_op jit(solution)/shard_map/rtk,rtc->kc/dot_general | solution.py:92
  111.5 42.1 %all-reduce = (f32[10,512]{1,0:T(8,128)}, f32[2,512]{1,0:T(2,128)S(1)}) all-reduce(f32[10,512]{1,0:T(8,128)S(1)} %fusion.8, f32[2,512]{1,0:T(2,128)S(1)} %pad_maximum_fusion.4), channel_id=1, replica_groups=mesh['rec'=4,'tm'=8] {'rec','tm'}, use_global_device_ids=true, to_apply=%region_8.0 | all-reduce | flops 6144 | bytes 49152 | tf_op jit(solution)/shard_map/psum | solution.py:94
  153.6 0.6 fusion.96
  154.2 82.8 %all-reduce.6.cloned.1.call-done = (f32[1536,512]{1,0:T(8,128)}, f32[1536,512]{1,0:T(8,128)}) async-done(((f32[1536,512]{1,0:T(8,128)}, f32[1536,512]{1,0:T(8,128)}), (f32[1536,512]{1,0:T(8,128)}, f32[1536,512]{1,0:T(8,128)})) %all-reduce.6.cloned.1.call-update) | async-done | bytes 6291472 | tf_op jit(solution)/shard_map/psum | solution.py:94
  237.0 4.0 %copy.33 = f32[1536,512]{1,0:T(8,128)} copy(f32[1536,512]{1,0:T(8,128)} %get-tuple-element.35) | data formatting | bytes 6291456
  241.1 1.7 copy.34
  (24 shorter events, 0.2 us)
Async XLA Ops:
  7.2 5.6 %copy-start = (f32[10,512]{1,0:T(8,128)S(1)}, f32[10,512]{1,0:T(8,128)}, u32[]{:S(2)}) copy-start(f32[10,512]{1,0:T(8,128)} %param.8) | copy-start | bytes 61444
  7.2 229.8 %all-reduce.6.cloned.1.call-start = ((), (), s32[]{:S(2)}) async-start(), calls=%async_computation | async-start | bytes 12582912 | tf_op jit(solution)/shard_map/psum | solution.py:94
  9.5 20.7 %copy-start.7 = (f32[512]{0:T(512)S(1)}, f32[512]{0:T(512)}, u32[]{:S(2)}) copy-start(f32[512]{0:T(512)} %param.9) | copy-start | bytes 6148
  9.5 20.7 %copy-start.8 = (f32[512]{0:T(512)S(1)}, f32[512]{0:T(512)}, u32[]{:S(2)}) copy-start(f32[512]{0:T(512)} %param.10) | copy-start | bytes 6148
  9.6 3.0 %collective-permute-start = (f32[1,1,5]{2,1,0:T(1,128)S(1)}, f32[1,1,5]{2,1,0:T(1,128)S(1)}, u32[]{:S(2)}, u32[]{:S(2)}) collective-permute-start(f32[1,1,5]{2,1,0:T(1,128)S(1)} %slice.85), channel_id=1, source_target_pairs={{1,0},{2,1},{3,2},{4,3},{5,4},{6,5},{7,6},{9,8},{10,9},{11,10},{12... | collective-permute-start | bytes 68 | tf_op jit(solution)/shard_map/ppermute | solution.py:13
  42.7 6.8 %collective-permute-start.1 = (bf16[1,1,512]{2,1,0:T(2,128)(2,1)S(1)}, bf16[1,1,512]{2,1,0:T(2,128)(2,1)S(1)}, u32[]{:S(2)}, u32[]{:S(2)}) collective-permute-start(bf16[1,1,512]{2,1,0:T(2,128)(2,1)S(1)} %slice.87), channel_id=1, source_target_pairs={{1,0},{2,1},{3,2},{4,3},{5,4},{6,5},{7,6},{9,8},{10,9},{11,10},{12... | collective-permute-start | bytes 3080 | tf_op jit(solution)/shard_map/ppermute | solution.py:13
  49.5 5.0 %copy-start.5 = (bf16[1,511,512]{2,1,0:T(8,128)(2,1)}, bf16[1,511,512]{2,1,0:T(8,128)(2,1)S(1)}, u32[]{:S(2)}) copy-start(bf16[1,511,512]{2,1,0:T(8,128)(2,1)S(1)} %slice.86) | copy-start | bytes 1569796
  54.6 5.9 %copy-start.9 = (bf16[1,256,512]{2,1,0:T(8,128)(2,1)S(1)}, bf16[1,256,512]{2,1,0:T(8,128)(2,1)}, u32[]{:S(2)}) copy-start(bf16[1,256,512]{2,1,0:T(8,128)(2,1)} %param.13) | copy-start | bytes 786436
  54.7 5.9 %collective-permute-start.2 = (bf16[1,1,512]{2,1,0:T(2,128)(2,1)S(1)}, bf16[1,1,512]{2,1,0:T(2,128)(2,1)S(1)}, u32[]{:S(2)}, u32[]{:S(2)}) collective-permute-start(bf16[1,1,512]{2,1,0:T(2,128)(2,1)S(1)} %slice.89), channel_id=1, source_target_pairs={{1,0},{2,1},{3,2},{4,3},{5,4},{6,5},{7,6},{9,8},{10,9},{11,10},{12... | collective-permute-start | bytes 3080 | tf_op jit(solution)/shard_map/ppermute | solution.py:13
  63.5 6.7 %collective-permute-start.3 = (bf16[1,1,512]{2,1,0:T(2,128)(2,1)S(1)}, bf16[1,1,512]{2,1,0:T(2,128)(2,1)S(1)}, u32[]{:S(2)}, u32[]{:S(2)}) collective-permute-start(bf16[1,1,512]{2,1,0:T(2,128)(2,1)S(1)} %slice.91), channel_id=1, source_target_pairs={{0,1},{1,2},{2,3},{3,4},{4,5},{5,6},{6,7},{8,9},{9,10},{10,11},{11... | collective-permute-start | bytes 3080 | tf_op jit(solution)/shard_map/ppermute | solution.py:13
  67.7 2.0 copy-start.3
  71.8 2.1 copy-start.1
  73.9 1.0 copy-start.6
  77.4 1.0 copy-start.4
  80.3 5.7 %collective-permute-start.4 = (bf16[1,1,512]{2,1,0:T(2,128)(2,1)S(1)}, bf16[1,1,512]{2,1,0:T(2,128)(2,1)S(1)}, u32[]{:S(2)}, u32[]{:S(2)}) collective-permute-start(bf16[1,1,512]{2,1,0:T(2,128)(2,1)S(1)} %slice.95), channel_id=1, source_target_pairs={{0,1},{1,2},{2,3},{3,4},{4,5},{5,6},{6,7},{8,9},{9,10},{10,11},{11... | collective-permute-start | bytes 3080 | tf_op jit(solution)/shard_map/ppermute | solution.py:13
  237.0 4.0 %copy-start.2 = (f32[1536,512]{1,0:T(8,128)S(1)}, f32[1536,512]{1,0:T(8,128)}, u32[]{:S(2)}) copy-start(f32[1536,512]{1,0:T(8,128)} %get-tuple-element.36) | copy-start | bytes 9437188
Sparse Core Ops, SparseCore 0:
  77.5 159.4 all-reduce.5
where the time goes:
time: 251 us; the launch traced here: 250 us
  waiting for transfers between devices  84.2 us (34%)
  blocking collectives  70.5 us (28%)
  other arithmetic  25.2 us (10%)
  matrix products  24.5 us (10%)
  local copies, waits for them, and re-layouts  19.4 us (8%)
  between operations  14.3 us (6%)
  starting transfers between devices  11.5 us (5%)
    psum x1, waiting for transfers between devices, shards(): lax.psum((grad_zero, norm_terms, grad_one, grad_two), ('rec', 'tm'))  82.8 us
    psum x1, blocking collectives, shards(): lax.psum((grad_zero, norm_terms, grad_one, grad_two), ('rec', 'tm'))  42.1 us
    psum x1, blocking collectives, shards(): lax.psum((jnp.sum(pre_norm, 1), jnp.sum(pre_norm * pre_norm, 1)), 'tm')  15.5 us
    psum x1, blocking collectives, shards(): sum_one, sum_two = lax.psum((local_one, local_two), 'tm')  12.9 us
    ppermute x5, starting transfers between devices, from_behind(): lax.ppermute(value, axis, [(source, source + steps) for source in range(l...  11.5 us
    convert_element_type x2, other arithmetic, shards(): act0 = jax.nn.gelu(shifted_norm, approximate=False).astype(jnp.bfloat16)  10.6 us
    unnamed x23, local copies, waits for them, and re-layouts  7.54 us
    dot_general x2, matrix products, stride_conv(): jnp.einsum('rtk,kc->rtc', following, weight[2 * channels:], preferred_ele...  7.41 us
  transfers between devices with their start and end apart: 6, of which 2 were waited for; matrix products, arithmetic and copies ran while one was open for 12% of the time, Pallas kernels for 0%

commit v1 on v0

--- a/solution.py
+++ b/solution.py
@@ -92,7 +92,7 @@
     grad_zero = jnp.einsum("rtk,rtc->kc", patches, dpre, precision=HIGH)
     norm_terms = jnp.stack([jnp.sum(local_two, 0), jnp.sum(local_one, 0)], 0)
     grad_zero, norm_terms, grad_one, grad_two = lax.psum(
-        (grad_zero, norm_terms, grad_one, grad_two), ("rec", "tm")
+        lax.psum((grad_zero, norm_terms, grad_one, grad_two), "tm"), "rec"
     )
     return (features, grad_zero, norm_terms[0], norm_terms[1], grad_one, grad_two)
 

time: 251 us -> 426 us (1.70)
  waiting for transfers between devices: 84.2 us -> 251 us
  blocking collectives: 70.5 us -> 81.4 us
    psum x1 -> x2, waiting for transfers between devices: 82.8 us -> 250 us  [the longest x1 142 us: shards(): lax.psum(lax.psum((grad_zero, norm_terms, grad_one, grad_two), 'tm'), 'rec')]
    psum x1 -> x2, blocking collectives: 42.1 us -> 51.3 us  [the longest x1 27 us: shards(): lax.psum(lax.psum((grad_zero, norm_terms, grad_one, grad_two), 'tm'), 'rec')]
  transfers between devices with their start and end apart: 6 -> 7, of which waited for: 2 -> 3; matrix products, arithmetic and copies ran while one was open for 12% -> 7% of each run, Pallas kernels for 0% -> 0%
where the time goes in v1:
time: 426 us; the launch traced here: 425 us
  waiting for transfers between devices  251 us (59%)
  blocking collectives  81.4 us (19%)
  other arithmetic  25 us (6%)
  matrix products  24.5 us (6%)
  local copies, waits for them, and re-layouts  19.4 us (5%)
  between operations  14.3 us (3%)
  starting transfers between devices  9.55 us (2%)
    psum x1, waiting for transfers between devices, shards(): lax.psum(lax.psum((grad_zero, norm_terms, grad_one, grad_two), 'tm'), 'rec')  142 us
    psum x1, waiting for transfers between devices, shards(): lax.psum((grad_zero, norm_terms, grad_one, grad_two), 'tm')  108 us
    psum x1, blocking collectives, shards(): lax.psum(lax.psum((grad_zero, norm_terms, grad_one, grad_two), 'tm'), 'rec')  27 us
    psum x1, blocking collectives, shards(): lax.psum((grad_zero, norm_terms, grad_one, grad_two), 'tm')  24.3 us
    psum x1, blocking collectives, shards(): lax.psum((jnp.sum(pre_norm, 1), jnp.sum(pre_norm * pre_norm, 1)), 'tm')  15.5 us
    psum x1, blocking collectives, shards(): sum_one, sum_two = lax.psum((local_one, local_two), 'tm')  14.6 us
    convert_element_type x2, other arithmetic, shards(): act0 = jax.nn.gelu(shifted_norm, approximate=False).astype(jnp.bfloat16)  10.6 us
    ppermute x5, starting transfers between devices, from_behind(): lax.ppermute(value, axis, [(source, source + steps) for source in range(l...  9.47 us
  transfers between devices with their start and end apart: 7, of which 3 were waited for; matrix products, arithmetic and copies ran while one was open for 7% of the time, Pallas kernels for 0%

profile of v1, /device:TPU:0, one launch (start us, length us, event | category | flops | bytes accessed | tf_op | source)
XLA Modules:
  0.0 425.0 jit_solution(10214376043737384646)
XLA Ops:
  7.2 0.0 copy-start
  7.2 0.0 all-reduce.9.cloned.1.call-start
  7.2 0.5 broadcast.213
  7.7 1.4 reduce.11
  9.2 0.4 reshape.355
  9.5 0.0 copy-start.7
  9.5 0.0 copy-start.8
  9.6 1.3 collective-permute-start
  10.9 0.2 copy.17
  11.1 0.2 copy.15
  11.3 1.3 collective-permute-done
  12.6 0.1 copy.16
  12.7 0.1 maximum_maximum_fusion
  12.8 1.9 fusion.93
  14.7 15.5 %all-reduce.2 = (f32[1,512]{1,0:T(1,128)S(1)}, f32[1,512]{1,0:T(1,128)S(1)}) all-reduce(f32[1,512]{1,0:T(1,128)S(1)} %bitcast.99, f32[1,512]{1,0:T(1,128)S(1)} %bitcast.98), channel_id=1, replica_groups=mesh['rec'=4,'tm'=8] {'tm'}, use_global_device_ids=true, to_apply=%region_3.0 | all-reduce | flops 1024 | bytes 8192 | tf_op jit(solution)/shard_map/psum | solution.py:66
  30.2 4.9 %fusion.2 = bf16[1024,512]{1,0:T(8,128)(2,1)S(1)} fusion(f32[1024,512]{1,0:T(8,128)S(1)} %get-tuple-element.28, f32[512]{0:T(512)S(1)} %copy-done.8, f32[512]{0:T(512)S(1)} %copy-done.7, f32[512]{0:T(512)S(1)} %bitcast.82, f32[512]{0:T(512)S(1)} %bitcast.86), kind=kLoop, calls=%fused_computation.6 | loop fusion | flops 36175872 | bytes 3153920 | tf_op jit(solution)/shard_map/convert_element_type | solution.py:73
  35.2 5.7 %fusion.106 = bf16[1,1024,512]{2,1,0:T(8,128)(2,1)} fusion(f32[512]{0:T(512)S(1)} %copy-done.8, f32[512]{0:T(512)S(1)} %copy-done.7, f32[512]{0:T(512)S(1)} %bitcast.83, f32[1024,512]{1,0:T(8,128)S(1)} %get-tuple-element.28, f32[512]{0:T(512)S(1)} %bitcast.87), kind=kLoop, calls=%fused_computation.151 | loop fusion | flops 36175872 | bytes 3153920 | tf_op jit(solution)/shard_map/convert_element_type | solution.py:73
  40.8 1.1 reshape.357
  42.0 0.7 slice.87
  42.7 1.3 collective-permute-start.1
  44.0 3.2 fusion.47
  47.2 1.1 reshape.358
  48.3 1.2 slice.86
  49.5 4.9 %fusion.24 = (bf16[512,512]{1,0:T(8,128)(2,1)S(1)}, f32[512,512]{1,0:T(8,128)}) fusion(f32[512,512]{1,0:T(8,128)} %fusion.47, bf16[1536,512]{1,0:T(8,128)(2,1)} %param.11, bf16[1,1,512]{2,1,0:T(2,128)(2,1)S(1)} %collective-permute-done.1, bf16[1,511,512]{2,1,0:T(8,128)(2,1)S(1)} %slice.86), kind=kOutput, calls=%fused_computation.49 | convolution fusion | flops 286785536 | bytes 3670016 | tf_op jit(solution)/shard_map/rtk,kc->rtc/dot_general | solution.py:31
  54.5 0.2 reshape.360
  54.7 1.4 collective-permute-start.2
  56.1 2.5 fusion.44
  58.6 1.0 reshape.361
  59.5 1.0 slice.88
  60.6 2.5 fusion.58
  63.1 0.5 fusion.77
  63.5 3.8 collective-permute-start.3
  67.4 0.3 fusion.75
  67.7 2.0 pad_maximum_fusion.1
  69.7 0.5 convolution_bitcast_fusion.2
  70.2 0.3 fusion.21
  70.6 0.1 pad_maximum_fusion.3
  70.7 1.2 reshape.365
  71.9 2.1 fusion.30
  73.9 0.7 fusion.97
  74.7 0.3 copy-done.6
  75.0 0.5 fusion.72
  75.4 2.0 pad_maximum_fusion
  77.4 0.0 all-reduce.9.cloned.1.call-update
  77.4 0.0 all-reduce.11.cloned.1.call-start
  77.5 107.6 %all-reduce.9.cloned.1.call-done = (f32[1536,512]{1,0:T(8,128)}, f32[1536,512]{1,0:T(8,128)}) async-done(((f32[1536,512]{1,0:T(8,128)}, f32[1536,512]{1,0:T(8,128)}), (f32[1536,512]{1,0:T(8,128)}, f32[1536,512]{1,0:T(8,128)})) %all-reduce.9.cloned.1.call-update) | async-done | bytes 6291472 | tf_op jit(solution)/shard_map/psum | solution.py:95
  185.1 0.0 all-reduce.11.cloned.1.call-update
  185.1 1.0 copy-done.4
  186.1 1.8 fusion.80
  187.9 1.6 collective-permute-start.4
  189.6 2.0 convolution_bitcast_fusion
  191.5 0.1 slice.97
  191.6 1.5 fusion.20
  193.2 1.5 pad_maximum_fusion.2
  194.6 2.7 reshape.367
  197.4 3.5 fusion.92
  200.9 14.6 %all-reduce.1 = (f32[1,512]{1,0:T(1,128)S(1)}, f32[1,512]{1,0:T(1,128)S(1)}) all-reduce(f32[1,512]{1,0:T(1,128)S(1)} %bitcast.93, f32[1,512]{1,0:T(1,128)S(1)} %bitcast.91), channel_id=1, replica_groups=mesh['rec'=4,'tm'=8] {'tm'}, use_global_device_ids=true, to_apply=%region_7.0 | all-reduce | flops 1024 | bytes 8192 | tf_op jit(solution)/shard_map/psum | solution.py:87
  215.5 3.1 fusion.8
  218.6 24.3 %all-reduce = (f32[10,512]{1,0:T(8,128)S(1)}, f32[2,512]{1,0:T(2,128)S(1)}) all-reduce(f32[10,512]{1,0:T(8,128)S(1)} %fusion.8, f32[2,512]{1,0:T(2,128)S(1)} %pad_maximum_fusion.4), channel_id=1, replica_groups=mesh['rec'=4,'tm'=8] {'tm'}, use_global_device_ids=true, to_apply=%region_8.0 | all-reduce | flops 6144 | bytes 49152 | tf_op jit(solution)/shard_map/psum | solution.py:95
  242.9 27.0 %all-reduce.4 = (f32[10,512]{1,0:T(8,128)}, f32[2,512]{1,0:T(2,128)S(1)}) all-reduce(f32[10,512]{1,0:T(8,128)S(1)} %get-tuple-element.10, f32[2,512]{1,0:T(2,128)S(1)} %get-tuple-element.11), channel_id=1, replica_groups=mesh['rec'=4,'tm'=8] {'rec'}, use_global_device_ids=true, to_apply=%region_9.0 | all-reduce | flops 6144 | bytes 49152 | tf_op jit(solution)/shard_map/psum | solution.py:94
  269.9 0.6 fusion.96
  270.5 142.0 %all-reduce.11.cloned.1.call-done = (f32[1536,512]{1,0:T(8,128)}, f32[1536,512]{1,0:T(8,128)}) async-done(((f32[1536,512]{1,0:T(8,128)}, f32[1536,512]{1,0:T(8,128)}), (f32[1536,512]{1,0:T(8,128)}, f32[1536,512]{1,0:T(8,128)})) %all-reduce.11.cloned.1.call-update) | async-done | bytes 6291472 | tf_op jit(solution)/shard_map/psum | solution.py:94
  412.5 4.0 copy.35
  416.5 1.7 copy.36
  (28 shorter events, 0.2 us)
Async XLA Ops:
  7.2 5.6 %copy-start = (f32[10,512]{1,0:T(8,128)S(1)}, f32[10,512]{1,0:T(8,128)}, u32[]{:S(2)}) copy-start(f32[10,512]{1,0:T(8,128)} %param.8) | copy-start | bytes 61444
  7.2 177.9 %all-reduce.9.cloned.1.call-start = ((), (), s32[]{:S(2)}) async-start(), calls=%async_computation | async-start | bytes 12582912 | tf_op jit(solution)/shard_map/psum | solution.py:95
  9.5 20.7 %copy-start.7 = (f32[512]{0:T(512)S(1)}, f32[512]{0:T(512)}, u32[]{:S(2)}) copy-start(f32[512]{0:T(512)} %param.9) | copy-start | bytes 6148
  9.5 20.7 %copy-start.8 = (f32[512]{0:T(512)S(1)}, f32[512]{0:T(512)}, u32[]{:S(2)}) copy-start(f32[512]{0:T(512)} %param.10) | copy-start | bytes 6148
  9.6 3.0 collective-permute-start
  42.7 6.8 %collective-permute-start.1 = (bf16[1,1,512]{2,1,0:T(2,128)(2,1)S(1)}, bf16[1,1,512]{2,1,0:T(2,128)(2,1)S(1)}, u32[]{:S(2)}, u32[]{:S(2)}) collective-permute-start(bf16[1,1,512]{2,1,0:T(2,128)(2,1)S(1)} %slice.87), channel_id=1, source_target_pairs={{1,0},{2,1},{3,2},{4,3},{5,4},{6,5},{7,6},{9,8},{10,9},{11,10},{12... | collective-permute-start | bytes 3080 | tf_op jit(solution)/shard_map/ppermute | solution.py:13
  49.5 5.0 %copy-start.5 = (bf16[1,511,512]{2,1,0:T(8,128)(2,1)}, bf16[1,511,512]{2,1,0:T(8,128)(2,1)S(1)}, u32[]{:S(2)}) copy-start(bf16[1,511,512]{2,1,0:T(8,128)(2,1)S(1)} %slice.86) | copy-start | bytes 1569796
  54.6 5.9 %copy-start.9 = (bf16[1,256,512]{2,1,0:T(8,128)(2,1)S(1)}, bf16[1,256,512]{2,1,0:T(8,128)(2,1)}, u32[]{:S(2)}) copy-start(bf16[1,256,512]{2,1,0:T(8,128)(2,1)} %param.13) | copy-start | bytes 786436
  54.7 5.9 %collective-permute-start.2 = (bf16[1,1,512]{2,1,0:T(2,128)(2,1)S(1)}, bf16[1,1,512]{2,1,0:T(2,128)(2,1)S(1)}, u32[]{:S(2)}, u32[]{:S(2)}) collective-permute-start(bf16[1,1,512]{2,1,0:T(2,128)(2,1)S(1)} %slice.89), channel_id=1, source_target_pairs={{1,0},{2,1},{3,2},{4,3},{5,4},{6,5},{7,6},{9,8},{10,9},{11,10},{12... | collective-permute-start | bytes 3080 | tf_op jit(solution)/shard_map/ppermute | solution.py:13
  63.5 6.7 %collective-permute-start.3 = (bf16[1,1,512]{2,1,0:T(2,128)(2,1)S(1)}, bf16[1,1,512]{2,1,0:T(2,128)(2,1)S(1)}, u32[]{:S(2)}, u32[]{:S(2)}) collective-permute-start(bf16[1,1,512]{2,1,0:T(2,128)(2,1)S(1)} %slice.91), channel_id=1, source_target_pairs={{0,1},{1,2},{2,3},{3,4},{4,5},{5,6},{6,7},{8,9},{9,10},{10,11},{11... | collective-permute-start | bytes 3080 | tf_op jit(solution)/shard_map/ppermute | solution.py:13
  67.7 2.0 copy-start.3
  71.9 2.1 copy-start.1
  73.9 1.0 copy-start.6
  77.4 335.1 %all-reduce.11.cloned.1.call-start = ((), (), s32[]{:S(2)}) async-start(), calls=%async_computation.1 | async-start | bytes 12582912 | tf_op jit(solution)/shard_map/psum | solution.py:94
  185.0 1.0 copy-start.4
  187.9 3.7 collective-permute-start.4
  412.5 4.0 copy-start.2
Sparse Core Ops, SparseCore 0:
  77.6 107.4 all-reduce.8
  187.6 224.8 all-reduce.10
